TPU v7x, 512 devices: a whole 4x8x8 slice. The times are simulated.
512 devices in a mesh: freq: 32 (over x_hi, y, core), rcv: 16 (over x_lo, z).
Axes of the slice: x: 4 (x_hi: 2, x_lo: 2; x = x_hi * 2 + x_lo), y: 8, z: 8, core: 2. Of those that a mesh axis runs over, the one named last changes fastest.
Arguments:
- direct_wave: float32 [32, 2048, 512], P('freq', 'rcv'), may hold values from -6 to 6
- reflection: bfloat16 [2, 64, 2048, 2048], P(None, 'freq', None, 'rcv'), may hold values from -0.0625 to 0.0625
- onset: int32 [32, 2048], P('freq', 'rcv'), may hold values from 64 to 447
Outputs:
- focus_plus: float32 [32, 2048, 512], P('freq', 'rcv')
- focus_minus: float32 [32, 2048, 512], P('freq', 'rcv')
All inputs are finite; a program needn't handle non-finite values.
Results may differ from a plain program's by a relative error of at most 0.013.
Values may be sent and summed in bfloat16 or wider, within the bound.
A program may use at most 64 MiB of HBM per device.

v0:
```python
import math

import jax
import jax.numpy as jnp
from jax import lax
from jax.sharding import PartitionSpec as P

NF = 64
NT = 512
ITERS = 2


HIGH = lax.Precision.HIGHEST


def tables():
    times = jnp.arange(NT, dtype=jnp.int32)
    bins = jnp.arange(NF, dtype=jnp.int32) + 1
    phase = times[:, None] * bins[None, :] % NT
    angle = phase.astype(jnp.float32) * (2.0 * math.pi / NT)
    return (jnp.cos(angle), jnp.sin(angle))


def spectrum(field, cosine, sine):
    real_part = jnp.einsum("pst,tk->kps", field, cosine, precision=HIGH)
    imag_part = -jnp.einsum("pst,tk->kps", field, sine, precision=HIGH)
    return jnp.stack([real_part, imag_part]).astype(jnp.bfloat16)


def trace(spec, cosine, sine, window):
    values = spec.astype(jnp.float32)
    field = jnp.einsum("kps,tk->pst", values[0], cosine, precision=HIGH) - jnp.einsum(
        "kps,tk->pst", values[1], sine, precision=HIGH
    )
    return field * (2.0 / NT) * window


def forward_product(spec, refl_rows):
    prods = jnp.einsum("cwps,dwrs->cdwpr", spec, refl_rows, preferred_element_type=jnp.float32)
    return jnp.stack([prods[0, 0] - prods[1, 1], prods[0, 1] + prods[1, 0]])


def adjoint_product(spec, refl_rows):
    prods = jnp.einsum("cwpr,dwrs->cdwps", spec, refl_rows, preferred_element_type=jnp.float32)
    return jnp.stack([prods[0, 0] + prods[1, 1], prods[1, 0] - prods[0, 1]])


def make_window(onset_part):
    return (jnp.arange(NT, dtype=jnp.int32)[None, None, :] < onset_part[:, :, None]).astype(
        jnp.float32
    )


def shards(direct_wave, reflection, onset):
    cosine, sine = tables()
    window = make_window(onset)
    focus_plus = direct_wave
    focus_minus = jnp.zeros_like(direct_wave)
    by_receiver = lax.all_to_all(reflection, "rcv", split_axis=2, concat_axis=3, tiled=True)
    for step in range(ITERS):
        plus_spec = lax.all_to_all(
            spectrum(focus_plus, cosine, sine), "freq", split_axis=1, concat_axis=2, tiled=True
        )
        upward = forward_product(
            lax.all_gather(plus_spec, "rcv", axis=3, tiled=True), by_receiver
        ).astype(jnp.bfloat16)
        upward_time = lax.all_to_all(upward, "freq", split_axis=2, concat_axis=1, tiled=True)
        focus_minus = trace(upward_time, cosine, sine, window)
        minus_spec = lax.all_to_all(
            spectrum(focus_minus, cosine, sine), "freq", split_axis=1, concat_axis=2, tiled=True
        )
        downward = adjoint_product(
            lax.all_gather(minus_spec, "rcv", axis=3, tiled=True), reflection
        )
        down_time = lax.all_to_all(
            downward.astype(jnp.bfloat16), "freq", split_axis=2, concat_axis=1, tiled=True
        )
        focus_plus = direct_wave + trace(down_time, cosine, sine, window)
    return (focus_plus, focus_minus)


def solution(mesh):
    return jax.shard_map(
        shards,
        mesh=mesh,
        in_specs=(P("freq", "rcv", None), P(None, "freq", None, "rcv"), P("freq", "rcv")),
        out_specs=(P("freq", "rcv", None), P("freq", "rcv", None)),
        check_vma=False,
    )
```

profile of v0, /device:TPU:1, one launch (start us, length us, event | category | flops | bytes accessed | tf_op | source)
XLA Modules:
  0.0 346.0 jit_solution(16774085853207993142)
XLA Ops:
  0.7 2.6 fusion.44
  3.3 2.4 fusion.37
  6.4 11.2 %all-to-all-start = ((bf16[2,64,1,128]{3,0,2,1:T(2,128)(2,1)}), bf16[2,64,1,128]{3,0,2,1:T(2,128)(2,1)S(1)}, u32[]{:S(2)}, u32[]{:S(2)}) async-start(bf16[2,64,1,128]{3,0,2,1:T(2,128)(2,1)} %copy.91), calls=%async_computation | async-start | bytes 65536 | tf_op jit(solution)/shard_map/all_to_all | solution.py:61
  17.6 14.0 %copy.94 = bf16[2,2,2048,128]{3,1,0,2:T(2,128)(2,1)} copy(bf16[2,2,2048,128]{3,2,1,0:T(8,128)(2,1)S(1)} %copy-done) | data formatting | bytes 4194304 | tf_op args[1]
  31.6 10.2 %all-to-all-start.1 = ((bf16[2,2,2048,128]{3,1,0,2:T(2,128)(2,1)}), bf16[2,2,2048,128]{3,1,0,2:T(2,128)(2,1)S(1)}, u32[]{:S(2)}, u32[]{:S(2)}) async-start(bf16[2,2,2048,128]{3,1,0,2:T(2,128)(2,1)} %copy.94), calls=%async_computation.1 | async-start | bytes 4194304 | tf_op jit(solution)/shard_map/all_to_all | solution.py:59
  41.8 70.9 %all-gather = bf16[2,2,32,1,2048]{4,2,0,1,3:T(8,128)(2,1)S(1)} all-gather(bf16[2,2,32,1,128]{4,2,0,1,3:T(8,128)(2,1)S(1)} %bitcast.216), channel_id=2, replica_groups=mesh['freq'=32,'rcv'=16] {'rcv'}, dimensions={4}, use_global_device_ids=true | all-gather | bytes 557056 | tf_op jit(solution)/shard_map/all_gather | solution.py:65
  112.7 2.7 copy.159
  115.4 2.8 reshape.436
  119.1 26.5 %all_to_all.150 = bf16[2,2,32,128]{3,1,0,2:T(2,128)(2,1)S(1)} all-to-all(bf16[2,2,32,128]{3,1,0,2:T(2,128)(2,1)S(1)} %copy.98), channel_id=1, replica_groups=mesh['freq'=32,'rcv'=16] {'freq'}, dimensions={2} | all-to-all | bytes 65536 | tf_op jit(solution)/shard_map/all_to_all | solution.py:67
  145.6 1.3 fusion.68
  146.9 1.3 fusion.17
  148.2 1.5 fusion.43
  149.7 1.5 fusion.38
  151.3 13.1 %all_to_all.151 = bf16[2,64,1,128]{3,0,2,1:T(2,128)(2,1)S(1)} all-to-all(bf16[2,64,1,128]{3,0,2,1:T(2,128)(2,1)S(1)} %copy.99), channel_id=1, replica_groups=mesh['freq'=32,'rcv'=16] {'freq'}, dimensions={1} | all-to-all | bytes 65536 | tf_op jit(solution)/shard_map/all_to_all | solution.py:69
  164.3 25.8 %all-gather.1 = bf16[2,2,32,1,2048]{4,2,0,1,3:T(8,128)(2,1)S(1)} all-gather(bf16[2,2,32,1,128]{4,2,0,1,3:T(8,128)(2,1)S(1)} %bitcast.217), channel_id=3, replica_groups=mesh['freq'=32,'rcv'=16] {'rcv'}, dimensions={4}, use_global_device_ids=true | all-gather | bytes 557056 | tf_op jit(solution)/shard_map/all_gather | solution.py:73
  190.7 20.2 %all_to_all.152 = bf16[2,2,32,128]{3,1,0,2:T(2,128)(2,1)S(1)} all-to-all(bf16[2,2,32,128]{3,1,0,2:T(2,128)(2,1)S(1)} %copy.105), channel_id=1, replica_groups=mesh['freq'=32,'rcv'=16] {'freq'}, dimensions={2} | all-to-all | bytes 65536 | tf_op jit(solution)/shard_map/all_to_all | solution.py:75
  210.9 1.3 fusion.65
  212.2 1.3 fusion.19
  213.5 1.5 fusion.42
  215.0 1.5 fusion.39
  216.6 13.1 %all_to_all.153 = bf16[2,64,1,128]{3,0,2,1:T(2,128)(2,1)S(1)} all-to-all(bf16[2,64,1,128]{3,0,2,1:T(2,128)(2,1)S(1)} %copy.106), channel_id=1, replica_groups=mesh['freq'=32,'rcv'=16] {'freq'}, dimensions={1} | all-to-all | bytes 65536 | tf_op jit(solution)/shard_map/all_to_all | solution.py:61
  229.6 26.7 %all-gather.2 = bf16[2,2,32,1,2048]{4,2,0,1,3:T(8,128)(2,1)S(1)} all-gather(bf16[2,2,32,1,128]{4,2,0,1,3:T(8,128)(2,1)S(1)} %bitcast.218), channel_id=4, replica_groups=mesh['freq'=32,'rcv'=16] {'rcv'}, dimensions={4}, use_global_device_ids=true | all-gather | bytes 557056 | tf_op jit(solution)/shard_map/all_gather | solution.py:65
  257.1 20.2 %all_to_all.154 = bf16[2,2,32,128]{3,1,0,2:T(2,128)(2,1)S(1)} all-to-all(bf16[2,2,32,128]{3,1,0,2:T(2,128)(2,1)S(1)} %copy.111), channel_id=1, replica_groups=mesh['freq'=32,'rcv'=16] {'freq'}, dimensions={2} | all-to-all | bytes 65536 | tf_op jit(solution)/shard_map/all_to_all | solution.py:67
  277.4 1.3 fusion.62
  278.7 1.3 fusion.12
  280.0 1.5 fusion.41
  281.5 1.5 fusion.40
  283.0 13.1 %all_to_all.155 = bf16[2,64,1,128]{3,0,2,1:T(2,128)(2,1)S(1)} all-to-all(bf16[2,64,1,128]{3,0,2,1:T(2,128)(2,1)S(1)} %copy.112), channel_id=1, replica_groups=mesh['freq'=32,'rcv'=16] {'freq'}, dimensions={1} | all-to-all | bytes 65536 | tf_op jit(solution)/shard_map/all_to_all | solution.py:69
  296.1 25.8 %all-gather.3 = bf16[2,2,32,1,2048]{4,2,0,1,3:T(8,128)(2,1)S(1)} all-gather(bf16[2,2,32,1,128]{4,2,0,1,3:T(8,128)(2,1)S(1)} %bitcast.219), channel_id=5, replica_groups=mesh['freq'=32,'rcv'=16] {'rcv'}, dimensions={4}, use_global_device_ids=true | all-gather | bytes 557056 | tf_op jit(solution)/shard_map/all_gather | solution.py:73
  322.5 20.2 %all_to_all.156 = bf16[2,2,32,128]{3,1,0,2:T(2,128)(2,1)S(1)} all-to-all(bf16[2,2,32,128]{3,1,0,2:T(2,128)(2,1)S(1)} %copy.118), channel_id=1, replica_groups=mesh['freq'=32,'rcv'=16] {'freq'}, dimensions={2} | all-to-all | bytes 65536 | tf_op jit(solution)/shard_map/all_to_all | solution.py:75
  342.7 1.3 fusion.59
  344.0 2.0 fusion.20
  (49 shorter events, 3.6 us)
Async XLA Ops:
  0.6 17.0 %copy-start = (bf16[2,2,2048,128]{3,2,1,0:T(8,128)(2,1)S(1)}, bf16[2,2,2048,128]{3,2,1,0:T(8,128)(2,1)}, u32[]{:S(2)}) copy-start(bf16[2,2,2048,128]{3,2,1,0:T(8,128)(2,1)} %param.4) | copy-start | bytes 6291460
  6.4 25.3 %all-to-all-start = ((bf16[2,64,1,128]{3,0,2,1:T(2,128)(2,1)}), bf16[2,64,1,128]{3,0,2,1:T(2,128)(2,1)S(1)}, u32[]{:S(2)}, u32[]{:S(2)}) async-start(bf16[2,64,1,128]{3,0,2,1:T(2,128)(2,1)} %copy.91), calls=%async_computation | async-start | bytes 65536 | tf_op jit(solution)/shard_map/all_to_all | solution.py:61
  31.6 81.1 %all-to-all-start.1 = ((bf16[2,2,2048,128]{3,1,0,2:T(2,128)(2,1)}), bf16[2,2,2048,128]{3,1,0,2:T(2,128)(2,1)S(1)}, u32[]{:S(2)}, u32[]{:S(2)}) async-start(bf16[2,2,2048,128]{3,1,0,2:T(2,128)(2,1)} %copy.94), calls=%async_computation.1 | async-start | bytes 4194304 | tf_op jit(solution)/shard_map/all_to_all | solution.py:59
  118.2 28.7 %copy-start.3 = (s32[1,128]{1,0:T(1,128)S(1)}, s32[1,128]{1,0:T(1,128)}, u32[]{:S(2)}) copy-start(s32[1,128]{1,0:T(1,128)} %param.5) | copy-start | bytes 1540
  146.9 43.2 %copy-start.1 = (bf16[2,2,2048,128]{3,2,1,0:T(8,128)(2,1)S(1)}, bf16[2,2,2048,128]{3,2,1,0:T(8,128)(2,1)}, u32[]{:S(2)}) copy-start(bf16[2,2,2048,128]{3,2,1,0:T(8,128)(2,1)} %param.4) | copy-start | bytes 6291460
  190.2 22.1 %copy-start.2 = (f32[1,128,512]{2,1,0:T(8,128)S(1)}, f32[1,128,512]{2,1,0:T(8,128)}, u32[]{:S(2)}) copy-start(f32[1,128,512]{2,1,0:T(8,128)} %param.3) | copy-start | bytes 786436
  279.9 42.4 %copy-start.4 = (f32[128,512]{1,0:T(8,128)}, f32[128,512]{1,0:T(8,128)S(1)}, u32[]{:S(2)}) copy-start(f32[128,512]{1,0:T(8,128)S(1)} %fusion.12) | copy-start | bytes 786436
where the time goes:
time: 347 us; the launch traced here: 346 us
  blocking collectives  276 us (80%)
  matrix products  27.3 us (8%)
  starting transfers between devices  21.4 us (6%)
  local copies, waits for them, and re-layouts  20.5 us (6%)
    all_gather x2, blocking collectives, shards(): lax.all_gather(plus_spec, 'rcv', axis=3, tiled=True)  97.6 us
    all_gather x2, blocking collectives, shards(): lax.all_gather(minus_spec, 'rcv', axis=3, tiled=True)  51.6 us
    all_to_all x2, blocking collectives, shards(): lax.all_to_all(upward, 'freq', split_axis=2, concat_axis=1, tiled=True)  46.7 us
    all_to_all x2, blocking collectives, shards(): lax.all_to_all(downward.astype(jnp.bfloat16), 'freq', split_axis=2, conca...  40.4 us
    all_to_all x2, blocking collectives, shards(): lax.all_to_all(spectrum(focus_minus, cosine, sine), 'freq', split_axis=1,...  26.1 us
    unnamed x11, local copies, waits for them, and re-layouts  14 us
    all_to_all x1, blocking collectives, shards(): lax.all_to_all(spectrum(focus_plus, cosine, sine), 'freq', split_axis=1,...  13.1 us
    all_to_all x1, starting transfers between devices, shards(): lax.all_to_all(spectrum(focus_plus, cosine, sine), 'freq', split_axis=1,...  11.2 us
  transfers between devices with their start and end apart: 2, of which 0 were waited for; matrix products, arithmetic and copies ran while one was open for 4% of the time, Pallas kernels for 0%

commit v1 on v0

v1 whole, which is shorter than its diff:
```python
import functools
import math

import jax
import jax.numpy as jnp
import ml_dtypes
import numpy as np
from jax import lax
from jax.experimental import pallas as pl
from jax.experimental.pallas import tpu as pltpu
from jax.sharding import PartitionSpec as P

NT = 512
ITERS = 2
BX = 128
F32 = jnp.float32
BF16 = jnp.bfloat16
MESH = pl.DeviceIdType.MESH


def tables(bins):
    phase = np.outer(np.arange(1, bins + 1), np.arange(NT)) % NT
    angle = phase.astype(np.float64) * (2.0 * math.pi / NT)
    rows = np.stack([np.cos(angle), -np.sin(angle)], axis=1).reshape(2 * bins, NT)
    high = rows.astype(ml_dtypes.bfloat16)
    low = (rows - high.astype(np.float64)).astype(ml_dtypes.bfloat16)
    to_bins = np.concatenate([high, low], axis=0)
    scale = ml_dtypes.bfloat16(2.0 / NT)
    to_time = np.concatenate([high.T * scale, low.T * scale], axis=1)
    return to_bins, to_time.astype(ml_dtypes.bfloat16)


def dot(a, b):
    return jnp.dot(a, b, preferred_element_type=F32)


def dot_nt(a, b):
    return lax.dot_general(a, b, (((1,), (1,)), ((), ())), preferred_element_type=F32)


def split(x):
    high = x.astype(BF16)
    return high, (x - high.astype(F32)).astype(BF16)


def kernel(
    nf, nr,
    wave_hbm, refl_hbm, onset_ref, bins_hbm, time_hbm,
    plus_ref, minus_ref,
    wave, refl, to_bins, to_time, first,
    a2a_out, a2a_in, rs_out, rs_in, ag,
    load_sem, a2a_send, a2a_recv, rs_send, rs_recv, ag_send, ag_recv,
):
    me_f = lax.axis_index("freq")
    me_r = lax.axis_index("rcv")
    rows = 4 * nf

    loads = [
        pltpu.make_async_copy(src, dst, load_sem.at[i])
        for i, (src, dst) in enumerate(
            ((wave_hbm.at[0], wave), (bins_hbm, to_bins), (time_hbm, to_time), (refl_hbm, refl))
        )
    ]
    for load in loads:
        load.start()

    barrier = pltpu.get_barrier_semaphore()

    def greet_f(j, _):
        pl.semaphore_signal(
            barrier, inc=1, device_id=(lax.rem(me_f + j, nf), me_r), device_id_type=MESH
        )
        return 0

    def greet_r(j, _):
        pl.semaphore_signal(
            barrier, inc=1, device_id=(me_f, lax.rem(me_r + j, nr)), device_id_type=MESH
        )
        return 0

    lax.fori_loop(1, nf, greet_f, 0)
    lax.fori_loop(1, nr, greet_r, 0)

    n_ids = lax.broadcasted_iota(jnp.int32, (rows, BX), 0)
    is_im = (n_ids % 2) == 1
    second = ((n_ids // 2) % 2) == 1
    onset = onset_ref[...]
    early = lax.broadcasted_iota(jnp.int32, (NT, BX), 0) < onset

    def exchange(stage, value):
        out, into = a2a_out.at[stage], a2a_in.at[stage]
        out[...] = value.reshape(nf, 4, BX)

        def push(j, _):
            to = lax.rem(me_f + j, nf)
            pltpu.make_async_remote_copy(
                src_ref=out.at[to], dst_ref=into.at[me_f],
                send_sem=a2a_send.at[stage], recv_sem=a2a_recv.at[stage],
                device_id=(to, me_r), device_id_type=MESH,
            ).start()
            return 0

        lax.fori_loop(1, nf, push, 0)
        pltpu.make_async_copy(out.at[me_f], into.at[me_f], a2a_recv.at[stage]).start()
        pltpu.make_async_copy(into, into, a2a_recv.at[stage]).wait()
        return into[...].reshape(rows, BX)

    def spectrum(field):
        high, low = split(field)
        both = dot(to_bins[...], high)
        return both[:rows] + both[rows:] + dot(to_bins[:rows], low)

    def trace(spec):
        both = jnp.concatenate([spec, spec], axis=0)
        return jnp.where(early, dot(to_time[...], both), 0.0)

    def turn(x):
        return jnp.where(is_im, jnp.roll(x, 1, axis=0), -jnp.roll(x, -1, axis=0))

    def forward(it, spec):
        spec = spec.astype(BF16).astype(F32)
        turned = turn(spec)
        weights = jnp.concatenate(
            [
                jnp.where(second, 0.0, spec), jnp.where(second, 0.0, turned),
                jnp.where(second, spec, 0.0), jnp.where(second, turned, 0.0),
            ],
            axis=1,
        ).astype(BF16)
        half = max(nr // 2, 1) * BX
        for part in range(nr * BX // half):
            rows_of = pl.ds(part * half, half)
            left = jnp.concatenate([refl[c, w, rows_of, :] for w in range(2) for c in range(2)], axis=1)
            block = dot_nt(left, weights).astype(BF16)
            rs_out[it, pl.ds(part * half // BX, half // BX)] = block.reshape(half // BX, BX, rows)

        def push(j, _):
            to = lax.rem(me_r + j, nr)
            pltpu.make_async_remote_copy(
                src_ref=rs_out.at[it, to], dst_ref=rs_in.at[it, me_r],
                send_sem=rs_send.at[it], recv_sem=rs_recv.at[it],
                device_id=(me_f, to), device_id_type=MESH,
            ).start()
            return 0

        lax.fori_loop(1, nr, push, 0)
        pltpu.make_async_copy(rs_out.at[it, me_r], rs_in.at[it, me_r], rs_recv.at[it]).start()
        pltpu.make_async_copy(rs_in.at[it], rs_in.at[it], rs_recv.at[it]).wait()
        total = rs_in[it, 0].astype(F32)
        for j in range(1, nr):
            total = total + rs_in[it, j].astype(F32)
        return total.T

    def adjoint(it, spec):
        ag[it, me_r] = spec.astype(BF16)

        def push(j, _):
            to = lax.rem(me_r + j, nr)
            pltpu.make_async_remote_copy(
                src_ref=ag.at[it, me_r], dst_ref=ag.at[it, me_r],
                send_sem=ag_send.at[it], recv_sem=ag_recv.at[it],
                device_id=(me_f, to), device_id_type=MESH,
            ).start()
            return 0

        lax.fori_loop(1, nr, push, 0)
        others = ag.at[it, pl.ds(0, nr - 1)]
        pltpu.make_async_copy(others, others, ag_recv.at[it]).wait()
        left = jnp.concatenate([ag[it, j] for j in range(nr)], axis=1)
        products = [
            dot(left, jnp.concatenate([refl[0, w], refl[1, w]], axis=1)) for w in range(2)
        ]
        product = jnp.where(
            jnp.concatenate([second, second], axis=1), products[1], products[0]
        )
        return product[:, :BX] - turn(product[:, BX:])

    loads[0].wait()
    loads[1].wait()
    high, low = split(wave[...])
    both = dot_nt(to_bins[...], high)
    first[...] = both[:rows] + both[rows:] + dot_nt(to_bins[:rows], low)
    loads[2].wait()

    pl.semaphore_wait(barrier, nf + nr - 2)
    onset_col = jnp.broadcast_to(onset, (BX, BX)).T

    def finish(spec):
        both = jnp.concatenate([spec.T, spec.T], axis=1).astype(BF16)
        field = dot(both, to_bins[...]) * (2.0 / NT)
        samples = lax.broadcasted_iota(jnp.int32, (BX, BX), 1)
        return [
            jnp.where(samples + k * BX < onset_col, field[:, k * BX:(k + 1) * BX], 0.0)
            for k in range(NT // BX)
        ]

    plus_spec = first[...]
    for it in range(ITERS):
        plus_bins = exchange(4 * it, plus_spec)
        if it == 0:
            loads[3].wait()
        upward = exchange(4 * it + 1, forward(it, plus_bins)).astype(BF16)
        minus_bins = exchange(4 * it + 2, spectrum(trace(upward)))
        if it == ITERS - 1:
            for k, part in enumerate(finish(upward.astype(F32))):
                minus_ref[0, :, pl.ds(k * BX, BX)] = part
        downward = exchange(4 * it + 3, adjoint(it, minus_bins)).astype(BF16)
        if it < ITERS - 1:
            plus_spec = first[...] + spectrum(trace(downward))
        else:
            for k, part in enumerate(finish(downward.astype(F32))):
                span = pl.ds(k * BX, BX)
                plus_ref[0, :, span] = wave[:, span] + part

    for stage in range(4 * ITERS):
        sent = a2a_out.at[stage, pl.ds(0, nf - 1)]
        pltpu.make_async_copy(sent, sent, a2a_send.at[stage]).wait()
    for it in range(ITERS):
        sent = rs_out.at[it, pl.ds(0, nr - 1)]
        pltpu.make_async_copy(sent, sent, rs_send.at[it]).wait()
        sent = ag.at[it, pl.ds(0, nr - 1)]
        pltpu.make_async_copy(sent, sent, ag_send.at[it]).wait()


def solution(mesh):
    nf, nr = mesh.shape["freq"], mesh.shape["rcv"]
    rows = 4 * nf
    to_bins, to_time = tables(2 * nf)

    def shards(direct_wave, reflection, onset):
        out = jax.ShapeDtypeStruct(direct_wave.shape, F32)
        anywhere = pl.BlockSpec(memory_space=pl.ANY)
        vmem = pl.BlockSpec(memory_space=pltpu.VMEM)
        return pl.pallas_call(
            functools.partial(kernel, nf, nr),
            out_shape=(out, out),
            in_specs=[anywhere, anywhere, vmem, anywhere, anywhere],
            out_specs=(vmem, vmem),
            scratch_shapes=[
                pltpu.VMEM(direct_wave.shape[1:], F32),
                pltpu.VMEM(reflection.shape, BF16),
                pltpu.VMEM(to_bins.shape, BF16),
                pltpu.VMEM(to_time.shape, BF16),
                pltpu.VMEM((rows, BX), F32),
                pltpu.VMEM((4 * ITERS, nf, 4, BX), F32),
                pltpu.VMEM((4 * ITERS, nf, 4, BX), F32),
                pltpu.VMEM((ITERS, nr, BX, rows), BF16),
                pltpu.VMEM((ITERS, nr, BX, rows), BF16),
                pltpu.VMEM((ITERS, nr, rows, BX), BF16),
                pltpu.SemaphoreType.DMA((4,)),
                pltpu.SemaphoreType.DMA((4 * ITERS,)),
                pltpu.SemaphoreType.DMA((4 * ITERS,)),
                pltpu.SemaphoreType.DMA((ITERS,)),
                pltpu.SemaphoreType.DMA((ITERS,)),
                pltpu.SemaphoreType.DMA((ITERS,)),
                pltpu.SemaphoreType.DMA((ITERS,)),
            ],
            compiler_params=pltpu.CompilerParams(
                collective_id=0, has_side_effects=True, vmem_limit_bytes=32 * 2**20
            ),
        )(direct_wave, reflection, onset, jnp.asarray(to_bins), jnp.asarray(to_time))

    return jax.shard_map(
        shards,
        mesh=mesh,
        in_specs=(P("freq", "rcv", None), P(None, "freq", None, "rcv"), P("freq", "rcv")),
        out_specs=(P("freq", "rcv", None), P("freq", "rcv", None)),
        check_vma=False,
    )
```

time: 347 us -> 136 us (0.39)
  blocking collectives: 276 us -> 0 us
  Pallas kernels: 0 us -> 129 us
  matrix products: 27.3 us -> 0 us
  starting transfers between devices: 21.4 us -> 0 us
  local copies, waits for them, and re-layouts: 20.5 us -> 6.49 us
    all_gather x4 -> x0, blocking collectives: 149 us -> none  [the longest x2 97.6 us: shards(): lax.all_gather(plus_spec, 'rcv', axis=3, tiled=True)]
    pallas_call x0 -> x1, Pallas kernels: none -> 129 us  [shards(): pl.pallas_call(functools.partial(kernel, nf, nr), out_shape=(out, out), i...]
    all_to_all x7 -> x0, blocking collectives: 126 us -> none  [the longest x2 46.7 us: shards(): lax.all_to_all(upward, 'freq', split_axis=2, concat_axis=1, tiled=True)]
    dot_general x20 -> x0, matrix products: 27.3 us -> none  [the longest x4 7.11 us: spectrum(): imag_part = -jnp.einsum('pst,tk->kps', field, sine, precision=HIGH)]
    all_to_all x2 -> x0, starting transfers between devices: 21.4 us -> none  [the longest x1 11.2 us: shards(): lax.all_to_all(spectrum(focus_plus, cosine, sine), 'freq', split_axis=1,...]
    unnamed x11 -> x12, local copies, waits for them, and re-layouts: 14 us -> 6.49 us
    all_to_all x6 -> x0, local copies, waits for them, and re-layouts: 5.53 us -> none  [the longest x2 5.5 us: shards(): lax.all_to_all(reflection, 'rcv', split_axis=2, concat_axis=3, tiled=True)]
  transfers between devices with their start and end apart: 2 -> 0, of which waited for: 0 -> 0; matrix products, arithmetic and copies ran while one was open for 4% -> 0% of each run, Pallas kernels for 0% -> 0%
where the time goes in v1:
time: 136 us
  Pallas kernels  129 us (95%)
  local copies, waits for them, and re-layouts  6.49 us (5%)
    pallas_call x1, Pallas kernels, shards(): pl.pallas_call(functools.partial(kernel, nf, nr), out_shape=(out, out), i...  129 us
    unnamed x12, local copies, waits for them, and re-layouts  6.49 us

profile of v1, /device:TPU:1, one launch (start us, length us, event | category | flops | bytes accessed | tf_op | source)
XLA Modules:
  0.0 135.9 jit_solution(11710181207264257721)
XLA Ops:
  0.6 0.0 copy-start
  0.6 1.6 %copy-done = bf16[2,2,2048,128]{3,2,1,0:T(8,128)(2,1)S(1)} copy-done((bf16[2,2,2048,128]{3,2,1,0:T(8,128)(2,1)S(1)}, bf16[2,2,2048,128]{3,2,1,0:T(8,128)(2,1)}, u32[]{:S(2)}) %copy-start) | copy-done | bytes 2097176
  2.2 0.0 copy-start.1
  2.2 0.9 copy-done.1
  3.2 0.0 copy-start.2
  3.2 0.9 copy-done.2
  4.1 0.0 copy-start.3
  4.1 0.9 copy-done.3
  5.1 0.0 copy-start.4
  5.1 0.7 copy-done.4
  5.7 128.7 %shard_map.68 = (f32[1,128,512]{2,1,0:T(8,128)S(1)}, f32[1,128,512]{2,1,0:T(8,128)S(1)}) custom-call(f32[1,128,512]{2,1,0:T(8,128)S(1)} %copy-done.1, bf16[2,2,2048,128]{3,2,1,0:T(8,128)(2,1)S(1)} %copy-done, s32[1,128]{1,0:T(1,128)S(1)} %copy-done.4, bf16[256,512]{1,0:T(8,128)(2,1)S(1)} %copy-done.3, bf16[512,256]{1,0:T(8,128)(2,1)S(1)} %copy-done.2), custom_call_target="tpu_custom_call" | custom-call | tf_op jit(solution)/shard_map/pallas_call | solution.py:234
  134.5 0.7 copy.9
  135.2 0.7 copy.10
Async XLA Ops:
  0.6 1.6 %copy-start = (bf16[2,2,2048,128]{3,2,1,0:T(8,128)(2,1)S(1)}, bf16[2,2,2048,128]{3,2,1,0:T(8,128)(2,1)}, u32[]{:S(2)}) copy-start(bf16[2,2,2048,128]{3,2,1,0:T(8,128)(2,1)} %refl_hbm.1) | copy-start | bytes 6291460
  2.2 0.9 copy-start.1
  3.2 0.9 copy-start.2
  4.1 0.9 copy-start.3
  5.1 0.7 copy-start.4

commit v2 on v1

v2 whole, which is shorter than its diff:
```python
import functools
import math

import jax
import jax.numpy as jnp
import ml_dtypes
import numpy as np
from jax import lax
from jax.experimental import pallas as pl
from jax.experimental.pallas import tpu as pltpu
from jax.sharding import PartitionSpec as P

NT = 512
ITERS = 2
BX = 128
GROUPS = 4
SUM_STRAIGHT = (0, 3)
GATHER_STRAIGHT = (3,)
SUM_ORDER = (0, 3, 1, 2)
GATHER_ORDER = (3, 0, 1, 2)
F32 = jnp.float32
BF16 = jnp.bfloat16
MESH = pl.DeviceIdType.MESH


def tables(bins):
    phase = np.outer(np.arange(1, bins + 1), np.arange(NT)) % NT
    angle = phase.astype(np.float64) * (2.0 * math.pi / NT)
    rows = np.stack([np.cos(angle), -np.sin(angle)], axis=1).reshape(2 * bins, NT)
    high = rows.astype(ml_dtypes.bfloat16)
    low = (rows - high.astype(np.float64)).astype(ml_dtypes.bfloat16)
    to_bins = np.concatenate([high, low], axis=0)
    scale = ml_dtypes.bfloat16(2.0 / NT)
    to_time = np.concatenate([high.T * scale, low.T * scale], axis=1)
    return to_bins, to_time.astype(ml_dtypes.bfloat16)


def dot(a, b):
    return jnp.dot(a, b, preferred_element_type=F32)


def dot_nt(a, b):
    return lax.dot_general(a, b, (((1,), (1,)), ((), ())), preferred_element_type=F32)


def split(x):
    high = x.astype(BF16)
    return high, (x - high.astype(F32)).astype(BF16)


def ring(n, k):
    return min(k % n, -k % n)


def offsets_freq(ny):
    steps = [(h, y, c) for h in range(2) for y in range(ny) for c in range(2)]
    return sorted(steps, key=lambda s: (ring(ny, s[1]) + 2 * s[0], -s[0], s[1], s[2]))


def offsets_rcv(nz):
    steps = [(h, z) for h in range(2) for z in range(nz)][1:]
    return sorted(steps, key=lambda s: (-ring(nz, s[1]) - s[0], s))


def kernel(
    nf, nr,
    wave_hbm, refl_hbm, onset_hbm, bins_hbm, time_hbm,
    plus_ref, minus_ref,
    wave, refl, onset_ref, turned_refl, to_bins, to_time, first,
    a2a_out, a2a_in, rs_out, rs_mate, rs_pair, rs_in, ag,
    load_sem, bins_send, bins_recv, time_send, time_recv, rs_send, rs_recv, ag_send, ag_recv,
    mate_send, mate_recv, relay_send, relay_recv,
):
    me_f = lax.axis_index("freq")
    me_r = lax.axis_index("rcv")
    rows = 4 * nf
    ny, nz = nf // 4, nr // 2
    near = offsets_freq(ny)
    back = [near.index((h, -y % ny, c)) for h, y, c in near]
    size = nf // GROUPS
    deep = 4 * size

    half, y_at, core = me_f // (2 * ny), (me_f // 2) % ny, me_f % 2
    freq_at = [
        (((half + h) % 2) * ny + (y_at + y) % ny) * 2 + (core + c) % 2 for h, y, c in near
    ]
    side, z_at = me_r // nz, me_r % nz
    rcv_at = [((side + h) % 2) * nz + (z_at + z) % nz for h, z in offsets_rcv(nz)]
    line_at = [side * nz + (z_at + z) % nz for h, z in offsets_rcv(nz) if h == 0]
    mate = (1 - side) * nz + z_at
    ours, theirs = pl.ds(side * nz, nz), pl.ds((1 - side) * nz, nz)

    loads = [
        pltpu.make_async_copy(src, dst, load_sem.at[i])
        for i, (src, dst) in enumerate(
            (
                (wave_hbm.at[0], wave), (bins_hbm, to_bins), (time_hbm, to_time),
                (refl_hbm, refl), (onset_hbm, onset_ref),
            )
        )
    ]
    for load in loads:
        load.start()

    barrier = pltpu.get_barrier_semaphore()
    for j in range(nf - 1, 0, -1):
        pl.semaphore_signal(barrier, inc=1, device_id=(freq_at[j], me_r), device_id_type=MESH)
    for to in rcv_at:
        pl.semaphore_signal(barrier, inc=1, device_id=(me_f, to), device_id_type=MESH)

    is_im = (lax.broadcasted_iota(jnp.int32, (rows, BX), 0) % 2) == 1
    second = ((lax.broadcasted_iota(jnp.int32, (rows, BX), 0) // 2) % 2) == 1
    group_im, group_second = is_im[:deep], second[:deep]
    def wait(ref, sem):
        pltpu.make_async_copy(ref, ref, sem).wait()

    def to_bin_owners(it, part, value):
        stage = 4 * it + 2 * part
        out, into = a2a_out.at[stage], a2a_in.at[stage]
        out[...] = value.reshape(nf, 4, BX)
        for j in range(nf - 1, 0, -1):
            pltpu.make_async_remote_copy(
                src_ref=out.at[freq_at[j]], dst_ref=into.at[back[j]],
                send_sem=bins_send.at[it, part], recv_sem=bins_recv.at[it, part, back[j] // size],
                device_id=(freq_at[j], me_r), device_id_type=MESH,
            ).start()
        into[0] = out[me_f]

    def from_time_owners(it, part, g):
        stage, least = 4 * it + 2 * part, 1 if g == 0 else 0
        if size > least:
            wait(
                a2a_in.at[stage, pl.ds(g * size + least, size - least)], bins_recv.at[it, part, g]
            )
        return a2a_in[stage, pl.ds(g * size, size)].reshape(deep, BX)

    def to_time_owners(it, part, g, value):
        stage = 4 * it + 2 * part + 1
        out, into = a2a_out.at[stage], a2a_in.at[stage]
        out[pl.ds(g * size, size)] = value.reshape(size, 4, BX)
        for j in range((g + 1) * size - 1, max(g * size, 1) - 1, -1):
            pltpu.make_async_remote_copy(
                src_ref=out.at[j], dst_ref=into.at[me_f],
                send_sem=time_send.at[it, part], recv_sem=time_recv.at[it, part],
                device_id=(freq_at[j], me_r), device_id_type=MESH,
            ).start()
        if g == 0:
            into[me_f] = out[0]

    def from_bin_owners(it, part):
        stage = 4 * it + 2 * part + 1
        wait(a2a_in.at[stage, pl.ds(0, nf - 1)], time_recv.at[it, part])
        return a2a_in[stage].reshape(rows, BX).astype(BF16)

    def spectrum(field):
        high, low = split(field)
        both = dot(to_bins[...], high)
        return both[:rows] + both[rows:] + dot(to_bins[:rows], low)

    def trace(spec):
        both = jnp.concatenate([spec, spec], axis=0)
        return jnp.where(early, dot(to_time[...], both), 0.0)

    def turn(x):
        return jnp.where(group_im, jnp.roll(x, 1, axis=0), -jnp.roll(x, -1, axis=0))

    def forward(it, g, spec):
        spec = spec.astype(BF16).astype(F32)
        turned = turn(spec)
        weights = jnp.concatenate(
            [
                jnp.where(group_second, 0.0, spec), jnp.where(group_second, 0.0, turned),
                jnp.where(group_second, spec, 0.0), jnp.where(group_second, turned, 0.0),
            ],
            axis=1,
        ).astype(BF16)
        for k in range(nr // 2):
            pair = dot(weights, turned_refl[:, pl.ds(2 * k * BX, 2 * BX)]).astype(BF16)
            rs_out[it, g, 2 * k] = pair[:, :BX]
            rs_out[it, g, 2 * k + 1] = pair[:, BX:]
        if g not in SUM_STRAIGHT:
            pltpu.make_async_remote_copy(
                src_ref=rs_out.at[it, g, theirs], dst_ref=rs_mate.at[it, g],
                send_sem=mate_send.at[it, g], recv_sem=mate_recv.at[it, g],
                device_id=(me_f, mate), device_id_type=MESH,
            ).start()
            return
        for j, to in enumerate(rcv_at):
            pltpu.make_async_remote_copy(
                src_ref=rs_out.at[it, g, to], dst_ref=rs_in.at[it, g, j],
                send_sem=rs_send.at[it, g], recv_sem=rs_recv.at[it, g],
                device_id=(me_f, to), device_id_type=MESH,
            ).start()

    def paired(it, g):
        wait(rs_mate.at[it, g], mate_recv.at[it, g])
        both = rs_out[it, g, ours].astype(F32) + rs_mate[it, g].astype(F32)
        rs_pair[it, g] = both.astype(BF16)
        for j, to in enumerate(line_at):
            pltpu.make_async_remote_copy(
                src_ref=rs_pair.at[it, g, to % nz], dst_ref=rs_in.at[it, g, j],
                send_sem=rs_send.at[it, g], recv_sem=rs_recv.at[it, g],
                device_id=(me_f, to), device_id_type=MESH,
            ).start()

    def summed(it, g):
        if g in SUM_STRAIGHT:
            terms, total = nr - 1, rs_out[it, g, me_r].astype(F32)
        else:
            terms, total = nz - 1, rs_pair[it, g, z_at].astype(F32)
        if terms:
            wait(rs_in.at[it, g, pl.ds(0, terms)], rs_recv.at[it, g])
        for j in range(terms):
            total = total + rs_in[it, g, j].astype(F32)
        return total

    def gather(it, g, spec):
        ag[it, g, me_r] = spec.astype(BF16)
        for to in rcv_at if g in GATHER_STRAIGHT else line_at:
            pltpu.make_async_remote_copy(
                src_ref=ag.at[it, g, me_r], dst_ref=ag.at[it, g, me_r],
                send_sem=ag_send.at[it, g], recv_sem=ag_recv.at[it, g],
                device_id=(me_f, to), device_id_type=MESH,
            ).start()

    def relay(it, g):
        if nz > 1:
            wait(ag.at[it, g, pl.ds(0, nz - 1)], ag_recv.at[it, g])
        pltpu.make_async_remote_copy(
            src_ref=ag.at[it, g, ours], dst_ref=ag.at[it, g, ours],
            send_sem=relay_send.at[it, g], recv_sem=relay_recv.at[it, g],
            device_id=(me_f, mate), device_id_type=MESH,
        ).start()

    def adjoint(it, g):
        if g in GATHER_STRAIGHT:
            wait(ag.at[it, g, pl.ds(0, nr - 1)], ag_recv.at[it, g])
        else:
            wait(ag.at[it, g, pl.ds(0, nz)], relay_recv.at[it, g])
        left = jnp.concatenate([ag[it, g, j] for j in range(nr)], axis=1)
        one, two = [dot(left, jnp.concatenate([refl[0, w], refl[1, w]], axis=1)) for w in range(2)]
        by_re = jnp.where(group_second, two[:, :BX], one[:, :BX])
        by_im = jnp.where(group_second, two[:, BX:], one[:, BX:])
        return by_re - turn(by_im)

    loads[0].wait()
    loads[1].wait()
    high, low = split(wave[...])
    both = dot_nt(to_bins[...], high)
    first[...] = both[:rows] + both[rows:] + dot_nt(to_bins[:rows], low)
    loads[2].wait()
    loads[4].wait()
    onset = onset_ref[...]
    early = lax.broadcasted_iota(jnp.int32, (NT, BX), 0) < onset
    onset_col = jnp.broadcast_to(onset, (BX, BX)).T

    def finish(spec):
        both = jnp.concatenate([spec.T, spec.T], axis=1).astype(BF16)
        field = dot(both, to_bins[...]) * (2.0 / NT)
        samples = lax.broadcasted_iota(jnp.int32, (BX, BX), 1)
        return [
            jnp.where(samples + k * BX < onset_col, field[:, k * BX:(k + 1) * BX], 0.0)
            for k in range(NT // BX)
        ]

    pl.semaphore_wait(barrier, nf + nr - 2)
    to_bin_owners(0, 0, first[...])
    loads[3].wait()
    for w in range(2):
        for c in range(2):
            for k in range(nr):
                block = refl[c, w, pl.ds(k * BX, BX), :]
                turned_refl[pl.ds((2 * w + c) * BX, BX), pl.ds(k * BX, BX)] = block.T
    for it in range(ITERS):
        for g in range(GROUPS):
            forward(it, g, from_time_owners(it, 0, g))
        for g in range(GROUPS):
            if g not in SUM_STRAIGHT:
                paired(it, g)
        for g in SUM_ORDER:
            to_time_owners(it, 0, g, summed(it, g))
        upward = from_bin_owners(it, 0)
        to_bin_owners(it, 1, spectrum(trace(upward)))
        if it == ITERS - 1:
            for k, part in enumerate(finish(upward.astype(F32))):
                minus_ref[0, :, pl.ds(k * BX, BX)] = part
        for g in range(GROUPS):
            gather(it, g, from_time_owners(it, 1, g))
        for g in range(GROUPS):
            if g not in GATHER_STRAIGHT:
                relay(it, g)
        for g in GATHER_ORDER:
            to_time_owners(it, 1, g, adjoint(it, g))
        downward = from_bin_owners(it, 1)
        if it < ITERS - 1:
            to_bin_owners(it + 1, 0, first[...] + spectrum(trace(downward)))
        else:
            for k, part in enumerate(finish(downward.astype(F32))):
                span = pl.ds(k * BX, BX)
                plus_ref[0, :, span] = wave[:, span] + part

    for it in range(ITERS):
        for part in range(2):
            stage = 4 * it + 2 * part
            wait(a2a_out.at[stage, pl.ds(0, nf - 1)], bins_send.at[it, part])
            wait(a2a_out.at[stage + 1, pl.ds(0, nf - 1)], time_send.at[it, part])
        for g in range(GROUPS):
            if g in SUM_STRAIGHT:
                wait(rs_out.at[it, g, pl.ds(0, nr - 1)], rs_send.at[it, g])
            else:
                wait(rs_out.at[it, g, theirs], mate_send.at[it, g])
                if nz > 1:
                    wait(rs_pair.at[it, g, pl.ds(0, nz - 1)], rs_send.at[it, g])
            if g in GATHER_STRAIGHT:
                wait(ag.at[it, g, pl.ds(0, nr - 1)], ag_send.at[it, g])
            else:
                wait(ag.at[it, g, ours], relay_send.at[it, g])
                if nz > 1:
                    wait(ag.at[it, g, pl.ds(0, nz - 1)], ag_send.at[it, g])


def solution(mesh):
    nf, nr = mesh.shape["freq"], mesh.shape["rcv"]
    rows, deep = 4 * nf, 4 * nf // GROUPS
    to_bins, to_time = tables(2 * nf)

    def shards(direct_wave, reflection, onset):
        out = pltpu.VMEM(direct_wave.shape, F32)
        in_hbm = [
            pltpu.with_memory_space_constraint(array, pltpu.HBM)
            for array in (direct_wave, reflection, onset, jnp.asarray(to_bins), jnp.asarray(to_time))
        ]
        anywhere = pl.BlockSpec(memory_space=pl.ANY)
        vmem = pl.BlockSpec(memory_space=pltpu.VMEM)
        dma = pltpu.SemaphoreType.DMA
        return pl.pallas_call(
            functools.partial(kernel, nf, nr),
            out_shape=(out, out),
            in_specs=[anywhere] * 5,
            out_specs=(vmem, vmem),
            scratch_shapes=[
                pltpu.VMEM(direct_wave.shape[1:], F32),
                pltpu.VMEM(reflection.shape, BF16),
                pltpu.VMEM(onset.shape, jnp.int32),
                pltpu.VMEM((4 * BX, nr * BX), BF16),
                pltpu.VMEM(to_bins.shape, BF16),
                pltpu.VMEM(to_time.shape, BF16),
                pltpu.VMEM((rows, BX), F32),
                pltpu.VMEM((4 * ITERS, nf, 4, BX), F32),
                pltpu.VMEM((4 * ITERS, nf, 4, BX), F32),
                pltpu.VMEM((ITERS, GROUPS, nr, deep, BX), BF16),
                pltpu.VMEM((ITERS, GROUPS, nr // 2, deep, BX), BF16),
                pltpu.VMEM((ITERS, GROUPS, nr // 2, deep, BX), BF16),
                pltpu.VMEM((ITERS, GROUPS, nr - 1, deep, BX), BF16),
                pltpu.VMEM((ITERS, GROUPS, nr, deep, BX), BF16),
                dma((5,)),
                dma((ITERS, 2)),
                dma((ITERS, 2, GROUPS)),
                dma((ITERS, 2)),
                dma((ITERS, 2)),
            ]
            + [dma((ITERS, GROUPS))] * 8,
            compiler_params=pltpu.CompilerParams(
                collective_id=0, has_side_effects=True, vmem_limit_bytes=32 * 2**20
            ),
        )(*in_hbm)

    return jax.shard_map(
        shards,
        mesh=mesh,
        in_specs=(P("freq", "rcv", None), P(None, "freq", None, "rcv"), P("freq", "rcv")),
        out_specs=(P("freq", "rcv", None), P("freq", "rcv", None)),
        check_vma=False,
    )
```

time: 136 us -> 106 us (0.78)
  Pallas kernels: 129 us -> 104 us
  local copies, waits for them, and re-layouts: 6.49 us -> 1.41 us
    pallas_call x1, Pallas kernels: 129 us -> 104 us  [shards(): pl.pallas_call(functools.partial(kernel, nf, nr), out_shape=(out, out), i...]
    unnamed x12 -> x2, local copies, waits for them, and re-layouts: 6.49 us -> 1.41 us
where the time goes in v2:
time: 106 us
  Pallas kernels  104 us (98%)
  local copies, waits for them, and re-layouts  1.41 us (1%)
    pallas_call x1, Pallas kernels, shards(): pl.pallas_call(functools.partial(kernel, nf, nr), out_shape=(out, out), i...  104 us

profile of v2, /device:TPU:1, one launch (start us, length us, event | category | flops | bytes accessed | tf_op | source)
XLA Modules:
  0.0 105.9 jit_solution(11168097152534898044)
XLA Ops:
  0.6 103.9 %shard_map.68 = (f32[1,128,512]{2,1,0:T(8,128)S(1)}, f32[1,128,512]{2,1,0:T(8,128)S(1)}) custom-call(f32[1,128,512]{2,1,0:T(8,128)} %wave_hbm.1, bf16[2,2,2048,128]{3,2,1,0:T(8,128)(2,1)} %refl_hbm.1, s32[1,128]{1,0:T(1,128)} %onset_hbm.1, bf16[256,512]{1,0:T(8,128)(2,1)} %constant.4.clone.bins_hbm, bf16[512,256]{1,0:T(8,128)(2,1)} %constant.5.clone.time_hbm), custom_call_target="tpu_custom_call" | custom-call | tf_op jit(solution)/shard_map/pallas_call | solution.py:336
  104.5 0.7 copy.9
  105.2 0.7 copy.10

commit v3 on v2

--- a/solution.py
+++ b/solution.py
@@ -17,7 +17,7 @@
 SUM_STRAIGHT = (0, 3)
 GATHER_STRAIGHT = (3,)
 SUM_ORDER = (0, 3, 1, 2)
-GATHER_ORDER = (3, 0, 1, 2)
+GATHER_SETS = ((3,), (0, 1, 2))
 F32 = jnp.float32
 BF16 = jnp.bfloat16
 MESH = pl.DeviceIdType.MESH
@@ -80,13 +80,16 @@
     size = nf // GROUPS
     deep = 4 * size
 
+    last = nf - max(size * GROUPS // 4, 1)
+    issue_order = [*range(nf - 1, last - 1, -1), *range(1, last)]
+
     half, y_at, core = me_f // (2 * ny), (me_f // 2) % ny, me_f % 2
     freq_at = [
         (((half + h) % 2) * ny + (y_at + y) % ny) * 2 + (core + c) % 2 for h, y, c in near
     ]
     side, z_at = me_r // nz, me_r % nz
-    rcv_at = [((side + h) % 2) * nz + (z_at + z) % nz for h, z in offsets_rcv(nz)]
-    line_at = [side * nz + (z_at + z) % nz for h, z in offsets_rcv(nz) if h == 0]
+    rcv_at = [(h, (side + h) % 2 * nz + (z_at + z) % nz) for h, z in offsets_rcv(nz)]
+    line_at = [to for h, to in rcv_at if h == 0]
     mate = (1 - side) * nz + z_at
     ours, theirs = pl.ds(side * nz, nz), pl.ds((1 - side) * nz, nz)
 
@@ -103,14 +106,16 @@
         load.start()
 
     barrier = pltpu.get_barrier_semaphore()
-    for j in range(nf - 1, 0, -1):
-        pl.semaphore_signal(barrier, inc=1, device_id=(freq_at[j], me_r), device_id_type=MESH)
-    for to in rcv_at:
-        pl.semaphore_signal(barrier, inc=1, device_id=(me_f, to), device_id_type=MESH)
+    peers = [(ring(ny, near[j][1]) + 2 * near[j][0], freq_at[j], me_r) for j in range(1, nf)]
+    peers += [
+        (ring(nz, z) + h, me_f, to) for (h, z), (_, to) in zip(offsets_rcv(nz), rcv_at)
+    ]
+    for _, f, r in sorted(peers, key=lambda peer: -peer[0]):
+        pl.semaphore_signal(barrier, inc=1, device_id=(f, r), device_id_type=MESH)
 
     is_im = (lax.broadcasted_iota(jnp.int32, (rows, BX), 0) % 2) == 1
     second = ((lax.broadcasted_iota(jnp.int32, (rows, BX), 0) // 2) % 2) == 1
-    group_im, group_second = is_im[:deep], second[:deep]
+    group_second = second[:deep]
     def wait(ref, sem):
         pltpu.make_async_copy(ref, ref, sem).wait()
 
@@ -118,7 +123,7 @@
         stage = 4 * it + 2 * part
         out, into = a2a_out.at[stage], a2a_in.at[stage]
         out[...] = value.reshape(nf, 4, BX)
-        for j in range(nf - 1, 0, -1):
+        for j in issue_order:
             pltpu.make_async_remote_copy(
                 src_ref=out.at[freq_at[j]], dst_ref=into.at[back[j]],
                 send_sem=bins_send.at[it, part], recv_sem=bins_recv.at[it, part, back[j] // size],
@@ -162,7 +167,7 @@
         return jnp.where(early, dot(to_time[...], both), 0.0)
 
     def turn(x):
-        return jnp.where(group_im, jnp.roll(x, 1, axis=0), -jnp.roll(x, -1, axis=0))
+        return jnp.where(is_im[:x.shape[0]], jnp.roll(x, 1, axis=0), -jnp.roll(x, -1, axis=0))
 
     def forward(it, g, spec):
         spec = spec.astype(BF16).astype(F32)
@@ -174,23 +179,27 @@
             ],
             axis=1,
         ).astype(BF16)
-        for k in range(nr // 2):
-            pair = dot(weights, turned_refl[:, pl.ds(2 * k * BX, 2 * BX)]).astype(BF16)
-            rs_out[it, g, 2 * k] = pair[:, :BX]
-            rs_out[it, g, 2 * k + 1] = pair[:, BX:]
-        if g not in SUM_STRAIGHT:
-            pltpu.make_async_remote_copy(
-                src_ref=rs_out.at[it, g, theirs], dst_ref=rs_mate.at[it, g],
-                send_sem=mate_send.at[it, g], recv_sem=mate_recv.at[it, g],
-                device_id=(me_f, mate), device_id_type=MESH,
-            ).start()
-            return
-        for j, to in enumerate(rcv_at):
-            pltpu.make_async_remote_copy(
-                src_ref=rs_out.at[it, g, to], dst_ref=rs_in.at[it, g, j],
-                send_sem=rs_send.at[it, g], recv_sem=rs_recv.at[it, g],
-                device_id=(me_f, to), device_id_type=MESH,
-            ).start()
+        for part in (1 - side, side):
+            for k in range(nz // 2):
+                at = part * nz + 2 * k
+                columns = pl.ds(pl.multiple_of(at * BX, 2 * BX), 2 * BX)
+                pair = dot(weights, turned_refl[:, columns]).astype(BF16)
+                rs_out[it, g, at] = pair[:, :BX]
+                rs_out[it, g, at + 1] = pair[:, BX:]
+            if g in SUM_STRAIGHT:
+                for j, (h, to) in enumerate(rcv_at):
+                    if (h == 0) == (part is side):
+                        pltpu.make_async_remote_copy(
+                            src_ref=rs_out.at[it, g, to], dst_ref=rs_in.at[it, g, j],
+                            send_sem=rs_send.at[it, g], recv_sem=rs_recv.at[it, g],
+                            device_id=(me_f, to), device_id_type=MESH,
+                        ).start()
+            elif part is not side:
+                pltpu.make_async_remote_copy(
+                    src_ref=rs_out.at[it, g, theirs], dst_ref=rs_mate.at[it, g],
+                    send_sem=mate_send.at[it, g], recv_sem=mate_recv.at[it, g],
+                    device_id=(me_f, mate), device_id_type=MESH,
+                ).start()
 
     def paired(it, g):
         wait(rs_mate.at[it, g], mate_recv.at[it, g])
@@ -216,7 +225,7 @@
 
     def gather(it, g, spec):
         ag[it, g, me_r] = spec.astype(BF16)
-        for to in rcv_at if g in GATHER_STRAIGHT else line_at:
+        for to in [to for h, to in rcv_at if h == 0 or g in GATHER_STRAIGHT]:
             pltpu.make_async_remote_copy(
                 src_ref=ag.at[it, g, me_r], dst_ref=ag.at[it, g, me_r],
                 send_sem=ag_send.at[it, g], recv_sem=ag_recv.at[it, g],
@@ -232,15 +241,19 @@
             device_id=(me_f, mate), device_id_type=MESH,
         ).start()
 
-    def adjoint(it, g):
-        if g in GATHER_STRAIGHT:
-            wait(ag.at[it, g, pl.ds(0, nr - 1)], ag_recv.at[it, g])
-        else:
-            wait(ag.at[it, g, pl.ds(0, nz)], relay_recv.at[it, g])
-        left = jnp.concatenate([ag[it, g, j] for j in range(nr)], axis=1)
+    def adjoint(it, groups):
+        for g in groups:
+            if g in GATHER_STRAIGHT:
+                wait(ag.at[it, g, pl.ds(0, nr - 1)], ag_recv.at[it, g])
+            else:
+                wait(ag.at[it, g, pl.ds(0, nz)], relay_recv.at[it, g])
+        left = jnp.concatenate(
+            [jnp.concatenate([ag[it, g, j] for j in range(nr)], axis=1) for g in groups], axis=0
+        )
         one, two = [dot(left, jnp.concatenate([refl[0, w], refl[1, w]], axis=1)) for w in range(2)]
-        by_re = jnp.where(group_second, two[:, :BX], one[:, :BX])
-        by_im = jnp.where(group_second, two[:, BX:], one[:, BX:])
+        lines = second[:deep * len(groups)]
+        by_re = jnp.where(lines, two[:, :BX], one[:, :BX])
+        by_im = jnp.where(lines, two[:, BX:], one[:, BX:])
         return by_re - turn(by_im)
 
     loads[0].wait()
@@ -289,8 +302,10 @@
         for g in range(GROUPS):
             if g not in GATHER_STRAIGHT:
                 relay(it, g)
-        for g in GATHER_ORDER:
-            to_time_owners(it, 1, g, adjoint(it, g))
+        for groups in GATHER_SETS:
+            values = adjoint(it, groups)
+            for k in range(len(groups) - 1, -1, -1):
+                to_time_owners(it, 1, groups[k], values[k * deep:(k + 1) * deep])
         downward = from_bin_owners(it, 1)
         if it < ITERS - 1:
             to_bin_owners(it + 1, 0, first[...] + spectrum(trace(downward)))
@@ -319,6 +334,17 @@
                     wait(ag.at[it, g, pl.ds(0, nz - 1)], ag_send.at[it, g])
 
 
+def put(plus_ref, minus_ref, plus_out, minus_out, sems):
+    copies = [
+        pltpu.make_async_copy(plus_ref, plus_out, sems.at[0]),
+        pltpu.make_async_copy(minus_ref, minus_out, sems.at[1]),
+    ]
+    for copy in copies:
+        copy.start()
+    for copy in copies:
+        copy.wait()
+
+
 def solution(mesh):
     nf, nr = mesh.shape["freq"], mesh.shape["rcv"]
     rows, deep = 4 * nf, 4 * nf // GROUPS
@@ -333,7 +359,7 @@
         anywhere = pl.BlockSpec(memory_space=pl.ANY)
         vmem = pl.BlockSpec(memory_space=pltpu.VMEM)
         dma = pltpu.SemaphoreType.DMA
-        return pl.pallas_call(
+        plus, minus = pl.pallas_call(
             functools.partial(kernel, nf, nr),
             out_shape=(out, out),
             in_specs=[anywhere] * 5,
@@ -364,6 +390,15 @@
                 collective_id=0, has_side_effects=True, vmem_limit_bytes=32 * 2**20
             ),
         )(*in_hbm)
+        shape = jax.ShapeDtypeStruct(direct_wave.shape, F32)
+        return pl.pallas_call(
+            put,
+            out_shape=(shape, shape),
+            in_specs=[vmem, vmem],
+            out_specs=(anywhere, anywhere),
+            scratch_shapes=[dma((2,))],
+            compiler_params=pltpu.CompilerParams(vmem_limit_bytes=2**20),
+        )(plus, minus)
 
     return jax.shard_map(
         shards,

time: 106 us -> 105 us (level)
  local copies, waits for them, and re-layouts: 1.41 us -> 0 us
    unnamed x2 -> x0, local copies, waits for them, and re-layouts: 1.41 us -> none
where the time goes in v3:
time: 105 us
  Pallas kernels  104 us (99%)
    pallas_call x1, Pallas kernels, shards(): pl.pallas_call(functools.partial(kernel, nf, nr), out_shape=(out, out), i...  103 us

profile of v3, /device:TPU:1, one launch (start us, length us, event | category | flops | bytes accessed | tf_op | source)
XLA Modules:
  0.0 104.6 jit_solution(3693081465988569172)
XLA Ops:
  0.6 103.2 %shard_map.68 = (f32[1,128,512]{2,1,0:T(8,128)S(1)}, f32[1,128,512]{2,1,0:T(8,128)S(1)}) custom-call(f32[1,128,512]{2,1,0:T(8,128)} %wave_hbm.1, bf16[2,2,2048,128]{3,2,1,0:T(8,128)(2,1)} %refl_hbm.1, s32[1,128]{1,0:T(1,128)} %onset_hbm.1, bf16[256,512]{1,0:T(8,128)(2,1)} %constant.4.clone.bins_hbm, bf16[512,256]{1,0:T(8,128)(2,1)} %constant.5.clone.time_hbm), custom_call_target="tpu_custom_call" | custom-call | tf_op jit(solution)/shard_map/pallas_call | solution.py:362
  103.8 0.8 shard_map.69

commit v4 on v3

--- a/solution.py
+++ b/solution.py
@@ -158,9 +158,8 @@
         return a2a_in[stage].reshape(rows, BX).astype(BF16)
 
     def spectrum(field):
-        high, low = split(field)
-        both = dot(to_bins[...], high)
-        return both[:rows] + both[rows:] + dot(to_bins[:rows], low)
+        both = dot(to_bins[...], field.astype(BF16))
+        return both[:rows] + both[rows:]
 
     def trace(spec):
         both = jnp.concatenate([spec, spec], axis=0)

time: 105 us -> 105 us (level)
  no operation moved by 1% of the time
where the time goes in v4:
time: 105 us; the launch traced here: 104 us
  Pallas kernels  104 us (99%)
    pallas_call x1, Pallas kernels, shards(): pl.pallas_call(functools.partial(kernel, nf, nr), out_shape=(out, out), i...  103 us

profile of v4, /device:TPU:1, one launch (start us, length us, event | category | flops | bytes accessed | tf_op | source)
XLA Modules:
  0.0 104.4 jit_solution(13164380975719679209)
XLA Ops:
  0.6 103.0 %shard_map.68 = (f32[1,128,512]{2,1,0:T(8,128)S(1)}, f32[1,128,512]{2,1,0:T(8,128)S(1)}) custom-call(f32[1,128,512]{2,1,0:T(8,128)} %wave_hbm.1, bf16[2,2,2048,128]{3,2,1,0:T(8,128)(2,1)} %refl_hbm.1, s32[1,128]{1,0:T(1,128)} %onset_hbm.1, bf16[256,512]{1,0:T(8,128)(2,1)} %constant.4.clone.bins_hbm, bf16[512,256]{1,0:T(8,128)(2,1)} %constant.5.clone.time_hbm), custom_call_target="tpu_custom_call" | custom-call | tf_op jit(solution)/shard_map/pallas_call | solution.py:361
  103.6 0.8 shard_map.69
